TPU v7x, 256 devices: a whole 4x4x8 slice. The times are simulated.
256 devices in a mesh: ctx: 32 (over x_hi, z, core), fsdp: 8 (over x_lo, y).
Axes of the slice: x: 4 (x_hi: 2, x_lo: 2; x = x_hi * 2 + x_lo), y: 4, z: 8, core: 2. Of those that a mesh axis runs over, the one named last changes fastest.
Arguments:
- hidden_states: bfloat16 [12288, 8192], P('ctx', 'fsdp'), may hold values from -6 to 6
- norm_gain: bfloat16 [8192], replicated, may hold values from 0.25 to 1.75
- qkv_weight: bfloat16 [8192, 8, 1280], P('ctx', 'fsdp')
- block_mask: int32 [64, 8, 10], P('ctx', 'fsdp'), may hold values 0 or 1
Outputs:
- attended: bfloat16 [12288, 8, 1024], P('ctx', 'fsdp')
All inputs are finite; a program needn't handle non-finite values. No bound on the sum of `block_mask` on one device may be relied on, other than what follows from the above.
Results may differ from a plain program's by a relative error of at most 0.008.
The roundings to bfloat16 on the way count: a program that leaves them out, or rounds other values in their place, can miss the bound.
Values may be sent and summed in bfloat16 or wider, within the bound.
A program may use at most 128 MiB of HBM per device.

v0:
```python
import jax
import jax.numpy as jnp
from jax import lax
from jax.sharding import PartitionSpec as P

HD = 128
STEPS = 4
RB = 128
QPG = 8


def passed_along(shard, axis, by):
    size = lax.axis_size(axis)
    pairs = [(i, i + by) for i in range(size) if 0 <= i + by < size]
    return lax.ppermute(shard, axis, pairs)


def rotary(values, position):
    halfway = values.shape[-1] // 2
    exponent = jnp.arange(0, 2 * halfway, 2).astype(jnp.float32) / (2 * halfway)
    inverse = jnp.power(jnp.float32(500000.0), -exponent)
    angles = position[:, None] * inverse[None, :]
    target = (angles.shape[0],) + (1,) * (values.ndim - 2) + (halfway,)
    cosine = jnp.cos(angles).reshape(target)
    sine_term = jnp.sin(angles).reshape(target)
    leading = values[..., :halfway]
    trailing = values[..., halfway:]
    return jnp.concatenate(
        [leading * cosine - trailing * sine_term, trailing * cosine + leading * sine_term], axis=-1
    )


def attend(queries, key_rows, value_rows, query_start, key_start, window):
    scores = jnp.einsum(
        "tgqd,kgd->gqtk", queries, key_rows, preferred_element_type=jnp.float32
    ) * HD ** (-0.5)
    query_position = query_start + jnp.arange(queries.shape[0], dtype=jnp.int32)
    key_position = key_start + jnp.arange(key_rows.shape[0], dtype=jnp.int32)
    allowed = (
        (key_position[None, :] <= query_position[:, None])
        & (key_position[None, :] > query_position[:, None] - window)
        & (key_position[None, :] >= 0)
    )
    scores = jnp.where(allowed[None, None], scores, -1e30)
    row_peak = jnp.max(scores, axis=-1, keepdims=True)
    exponent = jnp.exp(scores - row_peak)
    row_total = jnp.sum(exponent, axis=-1, keepdims=True)
    probs = (exponent / row_total).astype(jnp.bfloat16)
    output = jnp.einsum("gqtk,kgd->tgqd", probs, value_rows, preferred_element_type=jnp.float32)
    return output.astype(jnp.bfloat16).reshape(
        queries.shape[0], queries.shape[1], queries.shape[2] * queries.shape[3]
    )


def shards(hidden_states, norm_gain, qkv_weight, block_mask):
    tok_rows = hidden_states.shape[0]
    width_local = qkv_weight.shape[0]
    groups = qkv_weight.shape[1]
    query_width = QPG * HD
    cycle_index = lax.axis_index("ctx")
    gathered = lax.all_gather(hidden_states, "fsdp", axis=1, tiled=True)
    states = gathered.astype(jnp.float32)
    mean_square = jnp.mean(states * states, axis=1, keepdims=True)
    normed = (
        states * lax.rsqrt(mean_square + 1e-05) * norm_gain.astype(jnp.float32)[None, :]
    ).astype(jnp.bfloat16)
    shaped = qkv_weight.reshape(width_local // RB, RB, groups, QPG + 2, HD)
    masked = (shaped * block_mask.astype(jnp.bfloat16)[:, None, :, :, None]).reshape(
        width_local, groups, (QPG + 2) * HD
    )
    position = (cycle_index * tok_rows + jnp.arange(tok_rows, dtype=jnp.int32)).astype(jnp.float32)
    projected = jnp.einsum(
        "tr,rgc->tgc",
        normed,
        lax.all_gather(masked, "ctx", axis=0, tiled=True),
        preferred_element_type=jnp.float32,
    )
    pair_proj = projected[..., query_width:]
    rotated = rotary(pair_proj[..., :HD], position).astype(jnp.bfloat16)
    value_rows = pair_proj[..., HD:].astype(jnp.bfloat16)
    paired = jnp.stack([rotated, value_rows], axis=0)
    blocks = []
    current = paired
    for offset in range(STEPS):
        current = passed_along(current, "ctx", 1)
        blocks.append(current)
    window_pairs = jnp.concatenate(blocks[::-1] + [paired], axis=1)
    query_proj = projected[..., :query_width]
    queries = rotary(query_proj.reshape(tok_rows, groups, QPG, HD), position).astype(jnp.bfloat16)
    query_start = cycle_index * tok_rows
    return attend(
        queries,
        window_pairs[0],
        window_pairs[1],
        query_start,
        query_start - STEPS * tok_rows,
        STEPS * tok_rows,
    )


def solution(mesh):
    return jax.shard_map(
        shards,
        mesh=mesh,
        in_specs=(P("ctx", "fsdp"), P(), P("ctx", "fsdp", None), P("ctx", "fsdp", None)),
        out_specs=P("ctx", "fsdp", None),
        check_vma=False,
    )
```

profile of v0, /device:TPU:6, one launch (start us, length us, event | category | flops | bytes accessed | tf_op | source)
XLA Modules:
  0.0 362.1 jit_solution(1679910817942189413)
XLA Ops:
  6.5 0.0 copy-start.3
  6.5 0.0 all-gather.3.cloned.1.call-start
  6.5 0.7 all-gather.3.cloned.1.call-update
  7.3 0.0 all-gather.5.cloned.1.call-start
  7.3 0.7 convert_element_type.59
  8.0 0.1 copy.19
  8.1 0.4 mul.150
  8.5 0.4 mul.151
  8.9 1.3 copy.11
  10.3 1.0 mul.152
  11.3 0.0 all-gather.5.cloned.1.call-update
  11.3 0.0 copy-done.3
  11.4 1.4 and_and_fusion
  12.8 73.4 %all-gather.3.cloned.1.call-done = bf16[384,8192]{1,0:T(8,128)(2,1)} async-done(((bf16[384,1024]{1,0:T(8,128)(2,1)}), bf16[384,8192]{1,0:T(8,128)(2,1)}) %all-gather.3.cloned.1.call-update) | async-done | bytes 6291472 | tf_op jit(solution)/shard_map/all_gather | solution.py:61
  86.3 4.1 %fusion.4 = f32[384]{0:T(512)S(1)} fusion(bf16[384,8192]{1,0:T(8,128)(2,1)} %all-gather.3.cloned.1.call-done), kind=kLoop, calls=%fused_computation.9 | loop fusion | flops 9436800 | bytes 6292992 | tf_op jit(solution)/shard_map/reduce_sum | solution.py:63
  90.4 172.8 %all-gather.5.cloned.1.call-done = bf16[8192,1,1280]{0,2,1:T(8,128)(2,1)} async-done(((bf16[256,1,1280]{0,2,1:T(8,128)(2,1)}), bf16[8192,1,1280]{0,2,1:T(8,128)(2,1)}) %all-gather.5.cloned.1.call-update) | async-done | bytes 20971536 | tf_op jit(solution)/shard_map/all_gather | solution.py:75
  263.2 14.8 %fusion.12 = f32[384,1,1280]{2,0,1:T(8,128)} fusion(bf16[8192,1,1280]{0,2,1:T(8,128)(2,1)} %all-gather.5.cloned.1.call-done, bf16[384,8192]{1,0:T(8,128)(2,1)} %all-gather.3.cloned.1.call-done, f32[8192]{0:T(1024)S(1)} %convert_element_type.57, f32[384]{0:T(512)S(1)} %add_rsqrt_fusion), kind=kOutput, calls=%fused_computation.16 | convolution fusion | flops 8065646592 | bytes 29263360 | tf_op jit(solution)/shard_map/tr,rgc->tgc/dot_general | solution.py:72
  277.9 0.9 fusion.34
  278.9 1.9 fusion.36
  280.7 0.1 pad_maximum_fusion
  280.8 2.2 collective-permute-start
  283.0 0.8 multiply_cosine_fusion
  283.8 7.7 %collective-permute-done = bf16[2,384,1,128]{3,1,2,0:T(8,128)(2,1)S(1)} collective-permute-done((bf16[2,384,1,128]{3,1,2,0:T(8,128)(2,1)S(1)}, bf16[2,384,1,128]{3,1,2,0:T(8,128)(2,1)S(1)}, u32[]{:S(2)}, u32[]{:S(2)}) %collective-permute-start) | collective-permute-done | bytes 196640 | tf_op jit(solution)/shard_map/ppermute | solution.py:15
  291.4 1.9 collective-permute-start.1
  293.4 1.5 slice_bitcast_fusion
  294.9 0.3 copy.23
  295.2 6.8 %collective-permute-done.1 = bf16[2,384,1,128]{3,1,2,0:T(8,128)(2,1)S(1)} collective-permute-done((bf16[2,384,1,128]{3,1,2,0:T(8,128)(2,1)S(1)}, bf16[2,384,1,128]{3,1,2,0:T(8,128)(2,1)S(1)}, u32[]{:S(2)}, u32[]{:S(2)}) %collective-permute-start.1) | collective-permute-done | bytes 196640 | tf_op jit(solution)/shard_map/ppermute | solution.py:15
  302.0 1.9 collective-permute-start.2
  303.9 0.5 fusion.42
  304.4 8.2 %collective-permute-done.2 = bf16[2,384,1,128]{3,1,2,0:T(8,128)(2,1)S(1)} collective-permute-done((bf16[2,384,1,128]{3,1,2,0:T(8,128)(2,1)S(1)}, bf16[2,384,1,128]{3,1,2,0:T(8,128)(2,1)S(1)}, u32[]{:S(2)}, u32[]{:S(2)}) %collective-permute-start.2) | collective-permute-done | bytes 196640 | tf_op jit(solution)/shard_map/ppermute | solution.py:15
  312.6 2.1 collective-permute-start.3
  314.7 1.5 fusion.20
  316.2 7.0 %collective-permute-done.3 = bf16[2,384,1,128]{3,1,2,0:T(8,128)(2,1)S(1)} collective-permute-done((bf16[2,384,1,128]{3,1,2,0:T(8,128)(2,1)S(1)}, bf16[2,384,1,128]{3,1,2,0:T(8,128)(2,1)S(1)}, u32[]{:S(2)}, u32[]{:S(2)}) %collective-permute-start.3) | collective-permute-done | bytes 196640 | tf_op jit(solution)/shard_map/ppermute | solution.py:15
  323.3 0.1 constant_dynamic-update-slice_fusion
  323.5 0.0 copy-start.1
  323.5 0.9 copy-done.1
  324.4 5.4 %fusion.3 = (f32[8,384]{1,0:T(8,128)S(1)}, f32[1920,384,8]{1,0,2:T(8,128)S(1)}) fusion(pred[384,1920]{0,1:T(8,128)(4,1)S(1)} %and_and_fusion, bf16[384,8,64]{2,0,1:T(8,128)(2,1)} %get-tuple-element.6, bf16[384,8,64]{2,0,1:T(8,128)(2,1)S(1)} %get-tuple-element.5, bf16[2,1920,1,128]{3,1,2,0:T(8,128)(2,1)} %copy-done.1), kind=kOutput, calls=%fused_computation.6 | convolution fusion | flops 1529213952 | bytes 26013696 | tf_op jit(solution)/shard_map/tgqd,kgd->gqtk/dot_general | solution.py:34
  329.8 0.0 copy-start
  329.8 7.8 %copy-done = f32[1920,384,8]{1,0,2:T(8,128)} copy-done((f32[1920,384,8]{1,0,2:T(8,128)}, f32[1920,384,8]{1,0,2:T(8,128)S(1)}, u32[]{:S(2)}) %copy-start) | copy-done | bytes 23592984
  337.6 0.0 copy-start.2
  337.6 4.9 %fusion.2 = f32[8,384]{1,0:T(8,128)S(1)} fusion(f32[1920,384,8]{1,0,2:T(8,128)S(1)} %get-tuple-element.14, f32[8,384]{1,0:T(8,128)S(1)} %get-tuple-element.13, pred[384,1920]{0,1:T(8,128)(4,1)S(1)} %and_and_fusion), kind=kLoop, calls=%fused_computation.5 | loop fusion | flops 23589888 | bytes 24354816 | tf_op jit(solution)/shard_map/reduce_sum | solution.py:47
  342.6 0.0 copy-done.2
  342.6 11.5 %fusion.17 = bf16[128,8,384]{2,0,1:T(8,128)(2,1)S(1)} fusion(f32[8,384]{1,0:T(8,128)S(1)} %fusion.2, f32[8,384]{1,0:T(8,128)S(1)} %get-tuple-element.13, f32[1920,384,8]{1,0,2:T(8,128)} %copy-done, pred[384,1920]{0,1:T(8,128)(4,1)S(1)} %and_and_fusion, bf16[2,1920,1,128]{3,1,2,0:T(8,128)(2,1)S(1)} %copy-done.2), kind=kOutput, calls=%fused_computation.21 | convolution fusion | flops 1539833856 | bytes 25632768 | tf_op jit(solution)/shard_map/gqtk,kgd->tgqd/dot_general | solution.py:49
  354.0 1.2 copy.16
  (11 shorter events, 0.1 us)
Async XLA Ops:
  6.5 4.8 %copy-start.3 = (bf16[8192]{0:T(1024)(128)(2,1)S(1)}, bf16[8192]{0:T(1024)(128)(2,1)}, u32[]{:S(2)}) copy-start(bf16[8192]{0:T(1024)(128)(2,1)} %param.5) | copy-start | bytes 49156
  6.5 79.8 %all-gather.3.cloned.1.call-start = ((), (), s32[]{:S(2)}) async-start(), calls=%async_computation | async-start | bytes 7077888 | tf_op jit(solution)/shard_map/all_gather | solution.py:61
  7.3 255.9 %all-gather.5.cloned.1.call-start = ((), (), s32[]{:S(2)}) async-start(), calls=%async_computation.1 | async-start | bytes 21626880 | tf_op jit(solution)/shard_map/all_gather | solution.py:75
  280.8 10.6 %collective-permute-start = (bf16[2,384,1,128]{3,1,2,0:T(8,128)(2,1)S(1)}, bf16[2,384,1,128]{3,1,2,0:T(8,128)(2,1)S(1)}, u32[]{:S(2)}, u32[]{:S(2)}) collective-permute-start(bf16[2,384,1,128]{3,1,2,0:T(8,128)(2,1)S(1)} %pad_maximum_fusion), channel_id=1, source_target_pairs={{0,8},{8,16},{16,24},{24,32},{32,40},{40,48},{48,56},{56,64},{64,7... | collective-permute-start | bytes 589832 | tf_op jit(solution)/shard_map/ppermute | solution.py:15
  291.4 10.6 %collective-permute-start.1 = (bf16[2,384,1,128]{3,1,2,0:T(8,128)(2,1)S(1)}, bf16[2,384,1,128]{3,1,2,0:T(8,128)(2,1)S(1)}, u32[]{:S(2)}, u32[]{:S(2)}) collective-permute-start(bf16[2,384,1,128]{3,1,2,0:T(8,128)(2,1)S(1)} %collective-permute-done), channel_id=1, source_target_pairs={{0,8},{8,16},{16,24},{24,32},{32,40},{40,48},{48,56},{56,64},{64,7... | collective-permute-start | bytes 589832 | tf_op jit(solution)/shard_map/ppermute | solution.py:15
  302.0 10.6 %collective-permute-start.2 = (bf16[2,384,1,128]{3,1,2,0:T(8,128)(2,1)S(1)}, bf16[2,384,1,128]{3,1,2,0:T(8,128)(2,1)S(1)}, u32[]{:S(2)}, u32[]{:S(2)}) collective-permute-start(bf16[2,384,1,128]{3,1,2,0:T(8,128)(2,1)S(1)} %collective-permute-done.1), channel_id=1, source_target_pairs={{0,8},{8,16},{16,24},{24,32},{32,40},{40,48},{48,56},{56,64},{64,7... | collective-permute-start | bytes 589832 | tf_op jit(solution)/shard_map/ppermute | solution.py:15
  312.6 10.6 %collective-permute-start.3 = (bf16[2,384,1,128]{3,1,2,0:T(8,128)(2,1)S(1)}, bf16[2,384,1,128]{3,1,2,0:T(8,128)(2,1)S(1)}, u32[]{:S(2)}, u32[]{:S(2)}) collective-permute-start(bf16[2,384,1,128]{3,1,2,0:T(8,128)(2,1)S(1)} %collective-permute-done.2), channel_id=1, source_target_pairs={{0,8},{8,16},{16,24},{24,32},{32,40},{40,48},{48,56},{56,64},{64,7... | collective-permute-start | bytes 589832 | tf_op jit(solution)/shard_map/ppermute | solution.py:15
  323.5 0.9 copy-start.1
  329.8 7.8 %copy-start = (f32[1920,384,8]{1,0,2:T(8,128)}, f32[1920,384,8]{1,0,2:T(8,128)S(1)}, u32[]{:S(2)}) copy-start(f32[1920,384,8]{1,0,2:T(8,128)S(1)} %get-tuple-element.14) | copy-start | bytes 70778880
  337.6 4.9 %copy-start.2 = (bf16[2,1920,1,128]{3,1,2,0:T(8,128)(2,1)S(1)}, bf16[2,1920,1,128]{3,1,2,0:T(8,128)(2,1)}, u32[]{:S(2)}) copy-start(bf16[2,1920,1,128]{3,1,2,0:T(8,128)(2,1)} %copy-done.1) | copy-start | bytes 2949124
Sparse Core Ops, SparseCore 0:
  9.2 77.0 all-gather.2
  88.8 174.2 all-gather.4
where the time goes:
time: 362 us
  waiting for transfers between devices  277 us (77%)
  matrix products  31.6 us (9%)
  other arithmetic  16.5 us (5%)
  local copies, waits for them, and re-layouts  15.6 us (4%)
  between operations  13.6 us (4%)
  starting transfers between devices  8.12 us (2%)
    all_gather x1, waiting for transfers between devices, shards(): lax.all_gather(masked, 'ctx', axis=0, tiled=True)  173 us
    all_gather x1, waiting for transfers between devices, shards(): gathered = lax.all_gather(hidden_states, 'fsdp', axis=1, tiled=True)  73.4 us
    ppermute x4, waiting for transfers between devices, passed_along(): return lax.ppermute(shard, axis, pairs)  29.7 us
    dot_general x1, matrix products, shards(): jnp.einsum('tr,rgc->tgc', normed, lax.all_gather(masked, 'ctx', axis=0, t...  14.8 us
    unnamed x15, local copies, waits for them, and re-layouts  12 us
    dot_general x1, matrix products, attend(): jnp.einsum('gqtk,kgd->tgqd', probs, value_rows, preferred_element_type=jn...  11.5 us
    ppermute x4, starting transfers between devices, passed_along(): return lax.ppermute(shard, axis, pairs)  8.08 us
  transfers between devices with their start and end apart: 6, of which 6 were waited for; matrix products, arithmetic and copies ran while one was open for 4% of the time, Pallas kernels for 0%

commit v1 on v0

v1 whole, which is shorter than its diff:
```python
import jax
import jax.numpy as jnp
from jax import lax
from jax.experimental import pallas as pl
from jax.experimental.pallas import tpu as pltpu
from jax.sharding import PartitionSpec as P

MESH = pl.DeviceIdType.MESH
F32 = jnp.float32
BF16 = jnp.bfloat16
HD = 128
TOK = 384
WID = 1024
KH = 4096
ROWS = 256
NCH = 5
SUB = 48
NSUB = TOK // SUB
HALF = TOK // 2
STEPS = 4
WIN = STEPS * TOK + HD
NEG = -1e30
EXP_SCALE = HD ** (-0.5) * 1.4426950408889634


class Plan:
    def __init__(self):
        self.tasks = []
        self.waits = {}

    def token(self, name, wait=None):
        self.waits[name] = wait
        return name

    def add(self, name, deps, dur, prio, emit, sends=()):
        self.tasks.append((name, list(deps), dur, prio, emit, list(sends)))

    def order(self, start):
        ready = {name: 0.0 for name in start}
        free = {}
        now = 0.0
        left = list(self.tasks)
        done = []
        while left:
            best = None
            soonest = None
            for task in left:
                if all(d in ready for d in task[1]):
                    at = max([ready[d] for d in task[1]], default=0.0)
                    if at <= now:
                        if best is None or task[3] < best[3]:
                            best = task
                    elif soonest is None or at < soonest:
                        soonest = at
            if best is None:
                now = soonest
                continue
            left.remove(best)
            done.append(best)
            now += best[2]
            ready["done:" + best[0]] = now
            for link, dur, lat, token in best[5]:
                begin = max(now, free.get(link, 0.0))
                free[link] = begin + dur
                ready[token] = begin + dur + lat
        self.total = now
        return done

    def emit(self, start):
        waited = set()
        for name, deps, _, _, emit, _ in self.order(start):
            for d in deps:
                if d not in waited and self.waits.get(d) is not None:
                    self.waits[d]()
                waited.add(d)
            emit()


def body(
    x_hbm, g_ref, w_hbm, mask_ref, cos_hbm, sin_hbm, o_hbm,
    xv, wv, cosv, sinv, hid, nrm, wts, part, got, acc, qbuf, kvb, out, sq, tot, rs,
    in_s, wz_s, wz_r, ws_s, ws_r, hx_s, hx_r, hy_s, hy_r, sq_s, sq_r, tx_s, tx_r,
    pr_s, pr_r, kv_s, kv_r, o_s,
):
    ci = lax.axis_index("ctx")
    fi = lax.axis_index("fsdp")
    xh, z, c = ci // 16, (ci // 2) % 8, ci % 2
    xl, y = fi // 4, fi % 4
    inner = xh != xl

    def dev(xh_, z_, c_, xl_, y_):
        return (xh_ * 16 + z_ * 2 + c_, xl_ * 4 + y_)

    up = dev(xh, (z + 1) % 8, c, xl, y)
    down = dev(xh, (z + 7) % 8, c, xl, y)
    sib = dev(xh, z, 1 - c, xl, y)
    far = dev(1 - xh, z, c, xl, y)
    cross = dev(1 - xh, z, c, 1 - xl, y)
    side = dev(xh, z, c, 1 - xl, y)
    yup = dev(xh, z, c, xl, (y + 1) % 4)
    ydown = dev(xh, z, c, xl, (y + 3) % 4)
    after = ((ci + 2) % 32, fi)
    before = ((ci + 30) % 32, fi)
    peers = [(ci, (fi + k) % 8) for k in range(1, 8)]

    started = []

    def remote(src, dst, s, r, to):
        return pltpu.make_async_remote_copy(
            src_ref=src, dst_ref=dst, send_sem=s, recv_sem=r, device_id=to, device_id_type=MESH
        )

    def send(*args):
        cp = remote(*args)
        cp.start()
        started.append(cp)

    load_w = pltpu.make_async_copy(w_hbm, wv, in_s.at[0])
    load_x = pltpu.make_async_copy(x_hbm, xv, in_s.at[1])
    load_c = pltpu.make_async_copy(cos_hbm, cosv, in_s.at[2])
    load_n = pltpu.make_async_copy(sin_hbm, sinv, in_s.at[3])
    load_h = pltpu.make_async_copy(x_hbm, hid.at[1, y], in_s.at[4])
    load_w.start()
    load_x.start()
    load_c.start()
    load_n.start()

    @pl.when(jnp.logical_not(inner))
    def _():
        load_h.start()

    barrier = pltpu.get_barrier_semaphore()
    greeted = peers + [far, cross, up, down, sib, after, before]
    for d in greeted:
        pl.semaphore_signal(barrier, inc=1, device_id=d, device_id_type=MESH)

    load_w.wait()
    own_piece = z * 2 + c

    def piece(j, idx):
        return wts.at[j, pl.ds(pl.multiple_of(idx * ROWS, ROWS), ROWS)]

    for j in range(NCH):
        for half in range(2):
            head = 8 + half if j == 0 else 2 * (j - 1) + half
            for rb in range(2):
                keep = mask_ref[rb, head].astype(F32)
                block = wv[rb * 128:(rb + 1) * 128, head * 128:(head + 1) * 128].astype(F32)
                wts[j, pl.ds(pl.multiple_of(own_piece * ROWS + rb * 128, 128), 128), half * 128:(half + 1) * 128] = (
                    block * keep
                ).astype(BF16)
    load_x.wait()
    pl.semaphore_wait(barrier, len(greeted))

    def hrows(m):
        return pl.ds(m * SUB, SUB)

    first_to = (
        jnp.where(inner, cross[0], side[0]),
        jnp.where(inner, cross[1], side[1]),
    )
    first_t = jnp.where(inner, 0, 1)

    def first_send(m):
        send(xv.at[hrows(m)], hid.at[first_t, y, hrows(m)], hx_s.at[0, m], hx_r.at[first_t, m], first_to)

    def own_send(j):
        src = piece(j, own_piece)
        send(src, src, wz_s.at[j, 0, 0], wz_r.at[j, 0, 0], up)
        send(src, src, wz_s.at[j, 1, 0], wz_r.at[j, 1, 0], down)
        send(src, src, ws_s.at[j, 0], ws_r.at[j, 0], sib)

    first_send(0)
    own_send(0)
    first_send(1)
    own_send(1)
    for m in range(2, NSUB):
        first_send(m)

    @pl.when(jnp.logical_not(inner))
    def _():
        load_h.wait()

    lanes = jnp.zeros((TOK, 128), F32)
    for k in range(WID // 128):
        v = xv[:, k * 128:(k + 1) * 128].astype(F32)
        lanes = lanes + v * v
    sums = lax.dot_general(
        jnp.ones((8, 128), F32), lanes, (((1,), (1,)), ((), ())),
        precision=lax.Precision.HIGHEST, preferred_element_type=F32,
    )
    sq[fi] = sums
    for k in range(1, 8):
        send(sq.at[fi], sq.at[fi], sq_s.at[k - 1], sq_r.at[k - 1], peers[k - 1])

    plan = Plan()
    start = []

    def at(step):
        return ((z + 8 + step) % 8) * 2 + c

    pz, lz = 2.9, 1.5

    def wait_w(j, way, d):
        def go():
            if d < 3:
                ref = piece(j, at(-(d + 1) if way == 0 else d + 1))
            else:
                ref = wts.at[j, pl.ds(pl.multiple_of(at(4) * ROWS + way * 128, 128), 128)]
            remote(ref, ref, wz_s.at[j, way, d], wz_r.at[j, way, d], sib).wait_recv()
        return go

    def wait_s(j, k):
        def go():
            ref = wts.at[j, pl.ds(0, ROWS)]
            remote(ref, ref, ws_s.at[j, k], ws_r.at[j, k], sib).wait_recv()
        return go

    for j in range(NCH):
        for way in range(2):
            for d in range(4):
                plan.token(f"w{j}{way}{d}", wait_w(j, way, d))
        for k in range(8):
            plan.token(f"s{j}{k}", wait_s(j, k))

    def own_task(j):
        plan.add(
            f"own{j}", [f"done:w{j-2}02f", f"done:w{j-2}12f"] if j >= 2 else [], 0.3, 0,
            (lambda: own_send(j)) if j >= 2 else (lambda: None),
            [("zu", pz, lz, f"w{j}00"), ("zd", pz, lz, f"w{j}10"), ("cc", 0.6, 1.0, f"s{j}0")],
        )

    def fwd_task(j, way, d):
        def go():
            idx = at(-(d + 1) if way == 0 else d + 1)
            to = up if way == 0 else down
            if d < 2:
                src = piece(j, idx)
            else:
                src = wts.at[j, pl.ds(pl.multiple_of(idx * ROWS + way * 128, 128), 128)]
            send(src, src, wz_s.at[j, way, d + 1], wz_r.at[j, way, d + 1], to)
            src = piece(j, idx)
            k = 1 + way * 3 + d
            send(src, src, ws_s.at[j, k], ws_r.at[j, k], sib)
        link = "zu" if way == 0 else "zd"
        plan.add(
            f"w{j}{way}{d}f", [f"w{j}{way}{d}"], 0.2, 1, go,
            [(link, pz if d < 2 else pz / 2, lz, f"w{j}{way}{d+1}"), ("cc", 0.6, 1.0, f"s{j}{1+way*3+d}")],
        )

    def last_task(j):
        def go():
            src = piece(j, at(4))
            send(src, src, ws_s.at[j, 7], ws_r.at[j, 7], sib)
        plan.add(f"w{j}l", [f"w{j}03", f"w{j}13"], 0.1, 1, go, [("cc", 0.6, 1.0, f"s{j}7")])

    for j in range(NCH):
        own_task(j)
        for way in range(2):
            for d in range(3):
                fwd_task(j, way, d)
        last_task(j)
    chunk_in = [
        [f"s{j}{k}" for k in range(8)]
        + [f"done:w{j}{way}{d}f" for way in range(2) for d in range(3)]
        + [f"done:w{j}l"]
        for j in range(NCH)
    ]

    ph, lh = 2.2, 1.5

    def hpiece(t, yy, m):
        return hid.at[t, yy, hrows(m)]

    def wait_hx(t, m):
        ref = hpiece(t, y, m)
        remote(ref, ref, hx_s.at[0, m], hx_r.at[t, m], sib).wait_recv()

    def y_sends(t, m):
        ref = hpiece(t, y, m)
        send_when.append(remote(ref, ref, hy_s.at[t, m, 0], hy_r.at[t, m, 0], yup))
        send_when[-1].start()
        send_when.append(remote(ref, ref, hy_s.at[t, m, 1], hy_r.at[t, m, 1], ydown))
        send_when[-1].start()

    send_when = []
    y_links = lambda t, m: [("yu", ph, lh, f"y{t}{m}0"), ("yd", ph, lh, f"y{t}{m}1")]
    seq = [(1, 0), (0, 0), (1, 1), (0, 1)] + [(0, m) for m in range(2, NSUB)] + [(1, m) for m in range(2, NSUB)]
    rank = {tm: n for n, tm in enumerate(seq)}
    for m in range(NSUB):
        start.append(f"x1{m}")
        start.append(f"x0{m}")

    def x_in(m):
        def go():
            @pl.when(inner)
            def _():
                wait_hx(0, m)
                ref = hpiece(0, y, m)
                remote(ref, ref, hx_s.at[1, m], hx_r.at[0, m], side).start()
                y_sends(0, m)
        plan.add(f"xi0{m}", [f"xa0{m}"], 0.1, 2, go, [("xo", ph, lh, f"xb0{m}")])

    def x_out(m):
        def go():
            @pl.when(jnp.logical_not(inner))
            def _():
                wait_hx(0, m)
                y_sends(0, m)
        plan.add(f"xo0{m}", [f"xb0{m}"], 0.1, 2, go, y_links(0, m))

    def x_own(m):
        def go():
            @pl.when(inner)
            def _():
                wait_hx(1, m)
            y_sends(1, m)
        deps = [f"xc1{m}"] + ([f"done:xo0{NSUB-1}"] if m >= 2 else [])
        plan.add(f"xo1{m}", deps, 0.1, 3, go, y_links(1, m))

    plan.add(
        "first", [], 0.5, -1, lambda: None,
        [("xi", ph, lh, f"xa0{m}") for m in range(NSUB)] + [("xs", ph, lh, f"xc1{m}") for m in range(NSUB)],
    )
    for m in range(NSUB):
        x_in(m)
        x_out(m)
        x_own(m)

    def wait_y(t, m, k):
        def go():
            idx = (y + 3) % 4 if k == 0 else (y + 1) % 4 if k == 1 else (y + 2) % 4
            ref = hpiece(t, idx, m)
            remote(ref, ref, hy_s.at[t, m, k], hy_r.at[t, m, k], sib).wait_recv()
        return go

    def y_task(t, m):
        way = m % 2
        for k in range(3):
            plan.token(f"y{t}{m}{k}", wait_y(t, m, k))

        def go():
            ref = hpiece(t, (y + 3) % 4 if way == 0 else (y + 1) % 4, m)
            send(ref, ref, hy_s.at[t, m, 2], hy_r.at[t, m, 2], yup if way == 0 else ydown)
        plan.add(
            f"yf{t}{m}", [f"y{t}{m}{way}"], 0.1, 2, go, [("yu" if way == 0 else "yd", ph, lh, f"y{t}{m}2")]
        )

    def wait_sq(k):
        def go():
            remote(sq.at[0], sq.at[0], sq_s.at[k], sq_r.at[k], sib).wait_recv()
        return go

    def spread(which, rows8):
        inv = lax.rsqrt(rows8 * (1.0 / 8192.0) + 1e-05)
        rs[which] = lax.dot_general(
            inv, jnp.full((8, 128), 0.125, F32), (((0,), (0,)), ((), ())),
            precision=lax.Precision.HIGHEST, preferred_element_type=F32,
        )

    def total():
        rows8 = sq[0]
        for k in range(1, 8):
            rows8 = rows8 + sq[k]
        tot[1] = rows8
        send(tot.at[1], tot.at[0], tx_s.at[0], tx_r.at[0], far)
        spread(1, rows8)

    def wait_tx():
        remote(tot.at[1], tot.at[0], tx_s.at[0], tx_r.at[0], far).wait_recv()

    plan.token("tx", wait_tx)
    for k in range(7):
        start.append(plan.token(f"sq{k}", wait_sq(k)))
    plan.add("sqa", ["done:first"], 3.0, 0, lambda: None)
    plan.add("total", [f"sq{k}" for k in range(7)] + ["done:sqa"], 0.5, 1, total, [("none", 0, 2.5, "tx")])
    plan.add("other", ["tx"], 0.5, 1, lambda: spread(0, tot[0]))

    def norm_task(t, m, step, deps):
        def go():
            yy = (y + step) % 4
            gain = g_ref[pl.ds(xh * 4 + yy, 1), :]
            scale = rs[t, m * SUB:(m + 1) * SUB, :]
            for k in range(WID // 128):
                v = hid[t, yy, m * SUB:(m + 1) * SUB, k * 128:(k + 1) * 128].astype(F32)
                v = v * scale * gain[:, k * 128:(k + 1) * 128]
                nrm[t, m * SUB:(m + 1) * SUB, pl.ds(pl.multiple_of(yy * WID + k * 128, 128), 128)] = v.astype(BF16)
        plan.add(f"n{t}{m}{step}", deps + ["done:other" if t == 0 else "done:total"], 0.15, 4 + rank[(t, m)] * 0.01, go)

    for t in range(2):
        for m in range(NSUB):
            y_task(t, m)
            norm_task(t, m, 0, [f"done:xo{t}{m}"] + ([f"done:xi{t}{m}"] if t == 0 else []))
            norm_task(t, m, 3, [f"y{t}{m}0"])
            norm_task(t, m, 1, [f"y{t}{m}1"])
            norm_task(t, m, 2, [f"y{t}{m}2"])

    per_half = NSUB // 2

    def normed_in(t, h):
        return [f"done:n{t}{m}{s}" for m in range(h * per_half, (h + 1) * per_half) for s in range(4)]

    def product(t, h, j):
        return jnp.dot(nrm[t, h * HALF:(h + 1) * HALF, :], wts[j], preferred_element_type=F32)

    def wait_pr(j, h):
        def go():
            ref = got.at[j, pl.ds(h * HALF, HALF)]
            remote(ref, ref, pr_s.at[j, h], pr_r.at[j, h], far).wait_recv()
        return go

    def other_task(h, j):
        def go():
            rows = pl.ds(h * HALF, HALF)
            part[j, rows] = product(0, h, j)
            send(part.at[j, rows], got.at[j, rows], pr_s.at[j, h], pr_r.at[j, h], far)
        plan.token(f"p{j}{h}", wait_pr(j, h))
        plan.add(f"m0{h}{j}", normed_in(0, h) + chunk_in[j], 0.6, 5 + j * 0.1 + h * 0.01, go, [("xp", 4.4, 2.0, f"p{j}{h}")])

    def rotated(u, rows):
        return u * cosv[rows, :] + pltpu.roll(u, 64, 1) * sinv[rows, :]

    def own_product(h, j):
        def go():
            rows = pl.ds(h * HALF, HALF)
            acc[j, rows] = product(1, h, j)
        plan.add(f"m1{h}{j}", normed_in(1, h) + chunk_in[j], 0.6, 6 + j * 0.1 + h * 0.01, go)

    def kv_send(blk_from, blk_to, h, k, to):
        rows = pl.ds(h * HALF, HALF)
        send(kvb.at[blk_from, rows], kvb.at[blk_to, rows], kv_s.at[k, h], kv_r.at[k, h], to)

    def finish(h, j):
        def go():
            rows = pl.ds(h * HALF, HALF)
            u = acc[j, rows] + got[j, rows]
            left, right = u[:, :HD], u[:, HD:]
            if j == 0:
                kvb[4 + c, rows, 0:HD] = rotated(left, rows).astype(BF16)
                kvb[4 + c, rows, HD:2 * HD] = right.astype(BF16)
                kv_send(4 + c, 2 + c, h, 0, after)
                kv_send(4 + c, 4 + c, h, 2, sib)
            else:
                qbuf[j - 1, rows, 0:HD] = rotated(left, rows).astype(BF16)
                qbuf[j - 1, rows, HD:2 * HD] = rotated(right, rows).astype(BF16)
        sends = [("zu", 2.2, 2.0, f"k0{h}"), ("cc", 0.3, 1.0, f"k2{h}")] if j == 0 else []
        plan.add(f"f{h}{j}", [f"done:m1{h}{j}", f"p{j}{h}", "done:rope"], 0.3, 4.5 + j * 0.1, go, sends)

    def rope():
        load_c.wait()
        load_n.wait()

    plan.add("rope", [], 0.1, 20, rope)

    def wait_kv(k, h):
        def go():
            ref = kvb.at[0, pl.ds(0, HALF)]
            remote(ref, ref, kv_s.at[k, h], kv_r.at[k, h], sib).wait_recv()
        return go

    for h in range(2):
        for k in range(5):
            plan.token(f"k{k}{h}", wait_kv(k, h))

        def pass_one(h=h):
            kv_send(2 + c, c, h, 1, after)
            kv_send(2 + c, 2 + c, h, 3, sib)

        def pass_two(h=h):
            kv_send(c, c, h, 4, sib)

        plan.add(f"ka{h}", [f"k0{h}"], 0.1, 1, pass_one, [("zu", 2.2, 2.0, f"k1{h}"), ("cc", 0.3, 1.0, f"k3{h}")])
        plan.add(f"kb{h}", [f"k1{h}"], 0.1, 1, pass_two, [("cc", 0.3, 1.0, f"k4{h}")])
        for j in range(NCH):
            other_task(h, j)
            own_product(h, j)
            finish(h, j)
    window_in = [f"k{k}{h}" for k in (2, 3, 4) for h in range(2)] + [f"done:kb{h}" for h in range(2)] + [f"done:f{h}0" for h in range(2)]

    def attend(j):
        def go():
            row = lax.broadcasted_iota(jnp.int32, (HD, HD), 0)
            col = lax.broadcasted_iota(jnp.int32, (HD, HD), 1)
            later = col > row
            key_at = lax.broadcasted_iota(jnp.int32, (1, WIN), 1)

            def block(b, carry):
                r0 = pl.multiple_of(b * HD, HD)
                k0 = pl.multiple_of(c * TOK + b * HD, HD)
                keys = kvf[pl.ds(k0, WIN), 0:HD]
                vals = kvf[pl.ds(k0, WIN), HD:2 * HD]
                real = key_at >= (STEPS - ci) * TOK - b * HD
                for half in range(2):
                    q = qbuf[j - 1, pl.ds(r0, HD), half * HD:(half + 1) * HD]
                    s = lax.dot_general(q, keys, (((1,), (1,)), ((), ())), preferred_element_type=F32)
                    s = jnp.concatenate(
                        [
                            jnp.where(later, s[:, :HD], NEG),
                            s[:, HD:WIN - HD],
                            jnp.where(later, NEG, s[:, WIN - HD:]),
                        ],
                        axis=1,
                    )
                    s = jnp.where(real, s, NEG)
                    peak = jnp.max(s, axis=1, keepdims=True)
                    e = jnp.exp2((s - peak) * EXP_SCALE)
                    probs = (e * (1.0 / jnp.sum(e, axis=1, keepdims=True))).astype(BF16)
                    o = jnp.dot(probs, vals, preferred_element_type=F32)
                    out[j - 1, pl.ds(r0, HD), half * HD:(half + 1) * HD] = o.astype(BF16)
                return carry

            lax.fori_loop(0, TOK // HD, block, 0)
            pltpu.make_async_copy(out.at[j - 1], o_hbm.at[:, pl.ds((j - 1) * 256, 256)], o_s.at[j - 1]).start()
        plan.add(f"a{j}", window_in + [f"done:f{h}{j}" for h in range(2)], 3.0, 7 + j, go)

    kvf = kvb.reshape(6 * TOK, 2 * HD)
    for j in range(1, NCH):
        attend(j)

    plan.emit(start)
    body.total = plan.total

    for j in range(1, NCH):
        pltpu.make_async_copy(out.at[j - 1], o_hbm.at[:, pl.ds((j - 1) * 256, 256)], o_s.at[j - 1]).wait()
    for cp in started:
        cp.wait_send()
    for t in range(2):
        for m in range(NSUB):
            for k in range(2):
                ref = hpiece(t, y, m)
                remote(ref, ref, hy_s.at[t, m, k], hy_r.at[t, m, k], yup).wait_send()

    @pl.when(inner)
    def _():
        for m in range(NSUB):
            ref = hpiece(0, y, m)
            remote(ref, ref, hx_s.at[1, m], hx_r.at[0, m], side).wait_send()


def shards(hidden_states, norm_gain, qkv_weight, block_mask):
    ci = lax.axis_index("ctx")
    position = (ci * TOK + jnp.arange(TOK, dtype=jnp.int32)).astype(F32)
    inverse = jnp.power(F32(500000.0), -(jnp.arange(0, HD, 2).astype(F32) / HD))
    angles = position[:, None] * inverse[None, :]
    cosine, sine = jnp.cos(angles), jnp.sin(angles)
    cos2 = jnp.concatenate([cosine, cosine], axis=1)
    sin2 = jnp.concatenate([-sine, sine], axis=1)
    gain = norm_gain.astype(F32).reshape(8, WID)
    any_ = pl.BlockSpec(memory_space=pl.ANY)
    dma = pltpu.SemaphoreType.DMA
    result = pl.pallas_call(
        body,
        out_shape=jax.ShapeDtypeStruct((TOK, 1024), BF16),
        in_specs=[
            any_, pl.BlockSpec(memory_space=pltpu.VMEM), any_, pl.BlockSpec(memory_space=pltpu.SMEM), any_, any_,
        ],
        out_specs=any_,
        scratch_shapes=[
            pltpu.VMEM((TOK, WID), BF16),
            pltpu.VMEM((ROWS, 1280), BF16),
            pltpu.VMEM((TOK, HD), F32),
            pltpu.VMEM((TOK, HD), F32),
            pltpu.VMEM((2, 4, TOK, WID), BF16),
            pltpu.VMEM((2, TOK, KH), BF16),
            pltpu.VMEM((NCH, KH, 256), BF16),
            pltpu.VMEM((NCH, TOK, 256), F32),
            pltpu.VMEM((NCH, TOK, 256), F32),
            pltpu.VMEM((NCH, TOK, 256), F32),
            pltpu.VMEM((4, TOK, 256), BF16),
            pltpu.VMEM((6, TOK, 256), BF16),
            pltpu.VMEM((4, TOK, 256), BF16),
            pltpu.VMEM((8, 8, TOK), F32),
            pltpu.VMEM((2, 8, TOK), F32),
            pltpu.VMEM((2, TOK, HD), F32),
            dma((5,)),
            dma((NCH, 2, 4)), dma((NCH, 2, 4)),
            dma((NCH, 8)), dma((NCH, 8)),
            dma((2, NSUB)), dma((2, NSUB)),
            dma((2, NSUB, 3)), dma((2, NSUB, 3)),
            dma((7,)), dma((7,)),
            dma((1,)), dma((1,)),
            dma((NCH, 2)), dma((NCH, 2)),
            dma((5, 2)), dma((5, 2)),
            dma((4,)),
        ],
        compiler_params=pltpu.CompilerParams(
            collective_id=0, has_side_effects=True, vmem_limit_bytes=58 * 2**20
        ),
        cost_estimate=pl.CostEstimate(flops=12 * 10**9, bytes_accessed=3 * 10**6, transcendentals=6 * 10**6),
    )(
        hidden_states, gain, qkv_weight.reshape(ROWS, 1280), block_mask.reshape(2, 10), cos2, sin2,
    )
    return result.reshape(TOK, 1, 1024)


def solution(mesh):
    return jax.shard_map(
        shards,
        mesh=mesh,
        in_specs=(P("ctx", "fsdp"), P(), P("ctx", "fsdp", None), P("ctx", "fsdp", None)),
        out_specs=P("ctx", "fsdp", None),
        check_vma=False,
    )
```

time: 362 us -> 138 us (0.38)
  the two profiles are of different devices: /device:TPU:6 before, /device:TPU:1 now
where the time goes in v1:
time: 138 us
  Pallas kernels  132 us (96%)
  local copies, waits for them, and re-layouts  3.38 us (2%)
  other arithmetic  1.71 us (1%)
    pallas_call x1, Pallas kernels, shards(): pl.pallas_call(body, out_shape=jax.ShapeDtypeStruct((TOK, 1024), BF16), i...  132 us
    unnamed x3, local copies, waits for them, and re-layouts  2.76 us

profile of v1, /device:TPU:1, one launch (start us, length us, event | category | flops | bytes accessed | tf_op | source)
XLA Modules:
  0.0 137.5 jit_solution(16028237916869257660)
XLA Ops:
  0.0 0.0 copy-start
  0.0 0.7 copy-done
  0.7 0.6 reshape.33.g_ref
  1.3 0.8 fusion
  2.1 0.9 pad_maximum_fusion
  3.0 132.4 %shard_map.46 = bf16[384,1024]{1,0:T(8,128)(2,1)} custom-call(bf16[384,1024]{1,0:T(8,128)(2,1)} %x_hbm.1, f32[8,1024]{1,0:T(8,128)} %reshape.33.g_ref, bf16[256,1280]{1,0:T(8,128)(2,1)} %bitcast.4, s32[2,10]{1,0:T(2,128)} %bitcast.5, f32[384,128]{1,0:T(8,128)} %get-tuple-element.8.cos_hbm, f32[384,128]{1,0:T(8,128)} %get-tuple-element.9.sin_hbm), custom_call_target="tpu_custom_call" | custom-call | flops 12000000000 | bytes 3000000 | tf_op jit(solution)/shard_map/pallas_call | solution.py:551
  135.5 2.1 %copy.6 = bf16[384,1,1024]{2,0,1:T(8,128)(2,1)} copy(bf16[384,1,1024]{2,0,1:T(8,128)(2,1)} %bitcast.3) | data formatting | bytes 1572864
  (2 shorter events, 0.0 us)
Async XLA Ops:
  0.0 0.7 copy-start

commit v2 on v1

--- a/solution.py
+++ b/solution.py
@@ -150,36 +150,6 @@
                     block * keep
                 ).astype(BF16)
     load_x.wait()
-    pl.semaphore_wait(barrier, len(greeted))
-
-    def hrows(m):
-        return pl.ds(m * SUB, SUB)
-
-    first_to = (
-        jnp.where(inner, cross[0], side[0]),
-        jnp.where(inner, cross[1], side[1]),
-    )
-    first_t = jnp.where(inner, 0, 1)
-
-    def first_send(m):
-        send(xv.at[hrows(m)], hid.at[first_t, y, hrows(m)], hx_s.at[0, m], hx_r.at[first_t, m], first_to)
-
-    def own_send(j):
-        src = piece(j, own_piece)
-        send(src, src, wz_s.at[j, 0, 0], wz_r.at[j, 0, 0], up)
-        send(src, src, wz_s.at[j, 1, 0], wz_r.at[j, 1, 0], down)
-        send(src, src, ws_s.at[j, 0], ws_r.at[j, 0], sib)
-
-    first_send(0)
-    own_send(0)
-    first_send(1)
-    own_send(1)
-    for m in range(2, NSUB):
-        first_send(m)
-
-    @pl.when(jnp.logical_not(inner))
-    def _():
-        load_h.wait()
 
     lanes = jnp.zeros((TOK, 128), F32)
     for k in range(WID // 128):
@@ -190,8 +160,38 @@
         precision=lax.Precision.HIGHEST, preferred_element_type=F32,
     )
     sq[fi] = sums
+    pl.semaphore_wait(barrier, len(greeted))
     for k in range(1, 8):
         send(sq.at[fi], sq.at[fi], sq_s.at[k - 1], sq_r.at[k - 1], peers[k - 1])
+
+
+    def hrows(m):
+        return pl.ds(m * SUB, SUB)
+
+    first_to = (
+        jnp.where(inner, cross[0], side[0]),
+        jnp.where(inner, cross[1], side[1]),
+    )
+    first_t = jnp.where(inner, 0, 1)
+
+    def first_send(m):
+        send(xv.at[hrows(m)], hid.at[first_t, y, hrows(m)], hx_s.at[0, m], hx_r.at[first_t, m], first_to)
+
+    def own_send(j):
+        src = piece(j, own_piece)
+        send(src, src, wz_s.at[j, 0, 0], wz_r.at[j, 0, 0], up)
+        send(src, src, wz_s.at[j, 1, 0], wz_r.at[j, 1, 0], down)
+        send(src, src, ws_s.at[j, 0], ws_r.at[j, 0], sib)
+
+    first_send(0)
+    own_send(0)
+    first_send(1)
+    own_send(1)
+    first_send(2)
+
+    @pl.when(jnp.logical_not(inner))
+    def _():
+        load_h.wait()
 
     plan = Plan()
     start = []
@@ -287,9 +287,11 @@
     y_links = lambda t, m: [("yu", ph, lh, f"y{t}{m}0"), ("yd", ph, lh, f"y{t}{m}1")]
     seq = [(1, 0), (0, 0), (1, 1), (0, 1)] + [(0, m) for m in range(2, NSUB)] + [(1, m) for m in range(2, NSUB)]
     rank = {tm: n for n, tm in enumerate(seq)}
-    for m in range(NSUB):
-        start.append(f"x1{m}")
-        start.append(f"x0{m}")
+
+    def more(m):
+        if m + 3 < NSUB:
+            src = xv.at[hrows(m + 3)]
+            remote(src, hid.at[first_t, y, hrows(m + 3)], hx_s.at[0, m + 3], hx_r.at[first_t, m + 3], first_to).start()
 
     def x_in(m):
         def go():
@@ -299,7 +301,11 @@
                 ref = hpiece(0, y, m)
                 remote(ref, ref, hx_s.at[1, m], hx_r.at[0, m], side).start()
                 y_sends(0, m)
-        plan.add(f"xi0{m}", [f"xa0{m}"], 0.1, 2, go, [("xo", ph, lh, f"xb0{m}")])
+                more(m)
+        plan.add(
+            f"xi0{m}", [f"xa0{m}"], 0.1, 2, go,
+            [("xo", ph, lh, f"xb0{m}")] + ([("xi", ph, lh, f"xa0{m+3}")] if m + 3 < NSUB else []),
+        )
 
     def x_out(m):
         def go():
@@ -307,7 +313,11 @@
             def _():
                 wait_hx(0, m)
                 y_sends(0, m)
-        plan.add(f"xo0{m}", [f"xb0{m}"], 0.1, 2, go, y_links(0, m))
+                more(m)
+        plan.add(
+            f"xo0{m}", [f"xb0{m}"], 0.1, 2, go,
+            y_links(0, m) + ([("xs", ph, lh, f"xc1{m+3}")] if m + 3 < NSUB else []),
+        )
 
     def x_own(m):
         def go():
@@ -320,7 +330,7 @@
 
     plan.add(
         "first", [], 0.5, -1, lambda: None,
-        [("xi", ph, lh, f"xa0{m}") for m in range(NSUB)] + [("xs", ph, lh, f"xc1{m}") for m in range(NSUB)],
+        [("xi", ph, lh, f"xa0{m}") for m in range(3)] + [("xs", ph, lh, f"xc1{m}") for m in range(3)],
     )
     for m in range(NSUB):
         x_in(m)
@@ -529,6 +539,9 @@
             for k in range(2):
                 ref = hpiece(t, y, m)
                 remote(ref, ref, hy_s.at[t, m, k], hy_r.at[t, m, k], yup).wait_send()
+
+    for m in range(3, NSUB):
+        remote(xv.at[hrows(m)], hid.at[first_t, y, hrows(m)], hx_s.at[0, m], hx_r.at[first_t, m], first_to).wait_send()
 
     @pl.when(inner)
     def _():

time: 138 us -> 121 us (0.88)
  Pallas kernels: 132 us -> 116 us
    pallas_call x1, Pallas kernels: 132 us -> 116 us  [shards(): pl.pallas_call(body, out_shape=jax.ShapeDtypeStruct((TOK, 1024), BF16), i...]
where the time goes in v2:
time: 121 us
  Pallas kernels  116 us (96%)
  local copies, waits for them, and re-layouts  3.38 us (3%)
  other arithmetic  1.71 us (1%)
    pallas_call x1, Pallas kernels, shards(): pl.pallas_call(body, out_shape=jax.ShapeDtypeStruct((TOK, 1024), BF16), i...  116 us
    unnamed x3, local copies, waits for them, and re-layouts  2.76 us

profile of v2, /device:TPU:1, one launch (start us, length us, event | category | flops | bytes accessed | tf_op | source)
XLA Modules:
  0.0 121.0 jit_solution(9289097166432864302)
XLA Ops:
  0.0 0.0 copy-start
  0.0 0.7 copy-done
  0.7 0.6 reshape.33.g_ref
  1.3 0.8 fusion
  2.1 0.9 pad_maximum_fusion
  3.0 115.8 %shard_map.46 = bf16[384,1024]{1,0:T(8,128)(2,1)} custom-call(bf16[384,1024]{1,0:T(8,128)(2,1)} %x_hbm.1, f32[8,1024]{1,0:T(8,128)} %reshape.33.g_ref, bf16[256,1280]{1,0:T(8,128)(2,1)} %bitcast.4, s32[2,10]{1,0:T(2,128)} %bitcast.5, f32[384,128]{1,0:T(8,128)} %get-tuple-element.8.cos_hbm, f32[384,128]{1,0:T(8,128)} %get-tuple-element.9.sin_hbm), custom_call_target="tpu_custom_call" | custom-call | flops 12000000000 | bytes 3000000 | tf_op jit(solution)/shard_map/pallas_call | solution.py:564
  118.9 2.1 %copy.6 = bf16[384,1,1024]{2,0,1:T(8,128)(2,1)} copy(bf16[384,1,1024]{2,0,1:T(8,128)(2,1)} %bitcast.3) | data formatting | bytes 1572864
  (2 shorter events, 0.0 us)
Async XLA Ops:
  0.0 0.7 copy-start

commit v3 on v2

--- a/solution.py
+++ b/solution.py
@@ -20,6 +20,13 @@
 STEPS = 4
 WIN = STEPS * TOK + HD
 NEG = -1e30
+BACK = (2, 2, 2)
+EARLY = 0
+OWN = 1
+AHEAD = 3
+TGROUPS = (((0, 2), (2, 4), (4, 6), (6, 8)), ((0, 4), (4, 8)))
+QGROUPS = ((0, 4), (4, 8))
+KGROUPS = ((0, 4), (4, 6), (6, 8))
 EXP_SCALE = HD ** (-0.5) * 1.4426950408889634
 
 
@@ -77,10 +84,10 @@
 
 
 def body(
-    x_hbm, g_ref, w_hbm, mask_ref, cos_hbm, sin_hbm, o_hbm,
-    xv, wv, cosv, sinv, hid, nrm, wts, part, got, acc, qbuf, kvb, out, sq, tot, rs,
+    x_hbm, g_ref, w_hbm, mask_ref, cos_hbm, sin_hbm, o_ref,
+    xv, wv, half_c, half_n, cosv, sinv, hid, nrm, wts, part, got, acc, qbuf, kvb, sq, tot, rs,
     in_s, wz_s, wz_r, ws_s, ws_r, hx_s, hx_r, hy_s, hy_r, sq_s, sq_r, tx_s, tx_r,
-    pr_s, pr_r, kv_s, kv_r, o_s,
+    pr_s, pr_r, kv_s, kv_r,
 ):
     ci = lax.axis_index("ctx")
     fi = lax.axis_index("fsdp")
@@ -117,8 +124,8 @@
 
     load_w = pltpu.make_async_copy(w_hbm, wv, in_s.at[0])
     load_x = pltpu.make_async_copy(x_hbm, xv, in_s.at[1])
-    load_c = pltpu.make_async_copy(cos_hbm, cosv, in_s.at[2])
-    load_n = pltpu.make_async_copy(sin_hbm, sinv, in_s.at[3])
+    load_c = pltpu.make_async_copy(cos_hbm, half_c, in_s.at[2])
+    load_n = pltpu.make_async_copy(sin_hbm, half_n, in_s.at[3])
     load_h = pltpu.make_async_copy(x_hbm, hid.at[1, y], in_s.at[4])
     load_w.start()
     load_x.start()
@@ -186,7 +193,8 @@
     first_send(0)
     own_send(0)
     first_send(1)
-    own_send(1)
+    for j in range(1, BACK[2]):
+        own_send(j)
     first_send(2)
 
     @pl.when(jnp.logical_not(inner))
@@ -225,8 +233,8 @@
 
     def own_task(j):
         plan.add(
-            f"own{j}", [f"done:w{j-2}02f", f"done:w{j-2}12f"] if j >= 2 else [], 0.3, 0,
-            (lambda: own_send(j)) if j >= 2 else (lambda: None),
+            f"own{j}", [f"done:w{j-BACK[0]}{way}{BACK[1]}f" for way in range(2)] if j >= BACK[2] else [], 0.3, 0,
+            (lambda: own_send(j)) if j >= BACK[2] else (lambda: None),
             [("zu", pz, lz, f"w{j}00"), ("zd", pz, lz, f"w{j}10"), ("cc", 0.6, 1.0, f"s{j}0")],
         )
 
@@ -285,7 +293,7 @@
 
     send_when = []
     y_links = lambda t, m: [("yu", ph, lh, f"y{t}{m}0"), ("yd", ph, lh, f"y{t}{m}1")]
-    seq = [(1, 0), (0, 0), (1, 1), (0, 1)] + [(0, m) for m in range(2, NSUB)] + [(1, m) for m in range(2, NSUB)]
+    seq = [(0, m) for m in range(EARLY)] + [(1, m) for m in range(OWN)] + [(0, m) for m in range(EARLY, NSUB)] + [(1, m) for m in range(OWN, NSUB)]
     rank = {tm: n for n, tm in enumerate(seq)}
 
     def more(m):
@@ -300,7 +308,6 @@
                 wait_hx(0, m)
                 ref = hpiece(0, y, m)
                 remote(ref, ref, hx_s.at[1, m], hx_r.at[0, m], side).start()
-                y_sends(0, m)
                 more(m)
         plan.add(
             f"xi0{m}", [f"xa0{m}"], 0.1, 2, go,
@@ -312,11 +319,10 @@
             @pl.when(jnp.logical_not(inner))
             def _():
                 wait_hx(0, m)
-                y_sends(0, m)
                 more(m)
         plan.add(
             f"xo0{m}", [f"xb0{m}"], 0.1, 2, go,
-            y_links(0, m) + ([("xs", ph, lh, f"xc1{m+3}")] if m + 3 < NSUB else []),
+            [("xs", ph, lh, f"xc1{m+3}")] if m + 3 < NSUB else [],
         )
 
     def x_own(m):
@@ -324,9 +330,14 @@
             @pl.when(inner)
             def _():
                 wait_hx(1, m)
-            y_sends(1, m)
-        deps = [f"xc1{m}"] + ([f"done:xo0{NSUB-1}"] if m >= 2 else [])
-        plan.add(f"xo1{m}", deps, 0.1, 3, go, y_links(1, m))
+        plan.add(f"xo1{m}", [f"xc1{m}"], 0.1, 3, go)
+
+    def y_own(t, m):
+        n = rank[(t, m)]
+        deps = [f"done:xo{t}{m}"] + ([f"done:xi{t}{m}"] if t == 0 else [])
+        if n >= AHEAD:
+            deps.append("done:yf%d%d" % seq[n - AHEAD])
+        plan.add(f"ys{t}{m}", deps, 0.1, 1.5, lambda: y_sends(t, m), y_links(t, m))
 
     plan.add(
         "first", [], 0.5, -1, lambda: None,
@@ -336,6 +347,8 @@
         x_in(m)
         x_out(m)
         x_own(m)
+        for t in range(2):
+            y_own(t, m)
 
     def wait_y(t, m, k):
         def go():
@@ -395,7 +408,7 @@
                 v = hid[t, yy, m * SUB:(m + 1) * SUB, k * 128:(k + 1) * 128].astype(F32)
                 v = v * scale * gain[:, k * 128:(k + 1) * 128]
                 nrm[t, m * SUB:(m + 1) * SUB, pl.ds(pl.multiple_of(yy * WID + k * 128, 128), 128)] = v.astype(BF16)
-        plan.add(f"n{t}{m}{step}", deps + ["done:other" if t == 0 else "done:total"], 0.15, 4 + rank[(t, m)] * 0.01, go)
+        plan.add(f"n{t}{m}{step}", deps + ["done:other" if t == 0 else "done:total"], 0.05, 4 + rank[(t, m)] * 0.01, go)
 
     for t in range(2):
         for m in range(NSUB):
@@ -405,44 +418,63 @@
             norm_task(t, m, 1, [f"y{t}{m}1"])
             norm_task(t, m, 2, [f"y{t}{m}2"])
 
-    per_half = NSUB // 2
-
-    def normed_in(t, h):
-        return [f"done:n{t}{m}{s}" for m in range(h * per_half, (h + 1) * per_half) for s in range(4)]
-
-    def product(t, h, j):
-        return jnp.dot(nrm[t, h * HALF:(h + 1) * HALF, :], wts[j], preferred_element_type=F32)
+    def product(t, lo, hi, j):
+        return jnp.dot(nrm[t, lo * SUB:hi * SUB, :], wts[j], preferred_element_type=F32)
+
+    def sent(j):
+        return TGROUPS[0] if j < 2 else TGROUPS[1]
+
+    def sent_rows(j, h):
+        lo, hi = sent(j)[h]
+        return pl.ds(lo * SUB, (hi - lo) * SUB)
 
     def wait_pr(j, h):
         def go():
-            ref = got.at[j, pl.ds(h * HALF, HALF)]
+            ref = got.at[j, sent_rows(j, h)]
             remote(ref, ref, pr_s.at[j, h], pr_r.at[j, h], far).wait_recv()
         return go
 
     def other_task(h, j):
-        def go():
-            rows = pl.ds(h * HALF, HALF)
-            part[j, rows] = product(0, h, j)
+        lo, hi = sent(j)[h]
+
+        def go():
+            rows = sent_rows(j, h)
+            part[j, rows] = product(0, lo, hi, j)
             send(part.at[j, rows], got.at[j, rows], pr_s.at[j, h], pr_r.at[j, h], far)
         plan.token(f"p{j}{h}", wait_pr(j, h))
-        plan.add(f"m0{h}{j}", normed_in(0, h) + chunk_in[j], 0.6, 5 + j * 0.1 + h * 0.01, go, [("xp", 4.4, 2.0, f"p{j}{h}")])
+        deps = [f"done:n0{m}{s}" for m in range(lo, hi) for s in range(4)]
+        plan.add(
+            f"m0{h}{j}", deps + chunk_in[j], 1.0 if hi - lo > 2 else 0.7, 5 + j * 0.1 + h * 0.01, go,
+            [("xp", 1.1 * (hi - lo), 2.0, f"p{j}{h}")],
+        )
 
     def rotated(u, rows):
         return u * cosv[rows, :] + pltpu.roll(u, 64, 1) * sinv[rows, :]
 
+    def groups(j):
+        return KGROUPS if j == 0 else QGROUPS
+
     def own_product(h, j):
-        def go():
-            rows = pl.ds(h * HALF, HALF)
-            acc[j, rows] = product(1, h, j)
-        plan.add(f"m1{h}{j}", normed_in(1, h) + chunk_in[j], 0.6, 6 + j * 0.1 + h * 0.01, go)
+        lo, hi = groups(j)[h]
+
+        def go():
+            acc[j, pl.ds(lo * SUB, (hi - lo) * SUB)] = product(1, lo, hi, j)
+        deps = [f"done:n1{m}{s}" for m in range(lo, hi) for s in range(4)]
+        plan.add(f"m1{h}{j}", deps + chunk_in[j], 1.0 if hi - lo > 2 else 0.7, (4.4 if j == 0 else 6) + j * 0.1 + h * 0.01, go)
 
     def kv_send(blk_from, blk_to, h, k, to):
-        rows = pl.ds(h * HALF, HALF)
+        lo, hi = KGROUPS[h]
+        rows = pl.ds(lo * SUB, (hi - lo) * SUB)
         send(kvb.at[blk_from, rows], kvb.at[blk_to, rows], kv_s.at[k, h], kv_r.at[k, h], to)
 
+    def kv_time(h):
+        return 0.55 * (KGROUPS[h][1] - KGROUPS[h][0])
+
     def finish(h, j):
-        def go():
-            rows = pl.ds(h * HALF, HALF)
+        lo, hi = groups(j)[h]
+
+        def go():
+            rows = pl.ds(lo * SUB, (hi - lo) * SUB)
             u = acc[j, rows] + got[j, rows]
             left, right = u[:, :HD], u[:, HD:]
             if j == 0:
@@ -453,22 +485,27 @@
             else:
                 qbuf[j - 1, rows, 0:HD] = rotated(left, rows).astype(BF16)
                 qbuf[j - 1, rows, HD:2 * HD] = rotated(right, rows).astype(BF16)
-        sends = [("zu", 2.2, 2.0, f"k0{h}"), ("cc", 0.3, 1.0, f"k2{h}")] if j == 0 else []
-        plan.add(f"f{h}{j}", [f"done:m1{h}{j}", f"p{j}{h}", "done:rope"], 0.3, 4.5 + j * 0.1, go, sends)
+        sends = [("zu", kv_time(h), 2.0, f"k0{h}"), ("cc", 0.3, 1.0, f"k2{h}")] if j == 0 else []
+        parts = [p for p, (a, b) in enumerate(sent(j)) if a < hi and b > lo]
+        plan.add(
+            f"f{h}{j}", [f"done:m1{h}{j}", "done:rope"] + [f"p{j}{p}" for p in parts], 0.2, 4.5 + j * 0.1, go, sends
+        )
 
     def rope():
         load_c.wait()
         load_n.wait()
-
-    plan.add("rope", [], 0.1, 20, rope)
+        cosv[...] = jnp.concatenate([half_c[...], half_c[...]], axis=1)
+        sinv[...] = jnp.concatenate([-half_n[...], half_n[...]], axis=1)
+
+    plan.add("rope", ["done:other"], 0.5, 3.5, rope)
 
     def wait_kv(k, h):
         def go():
-            ref = kvb.at[0, pl.ds(0, HALF)]
+            ref = kvb.at[0, pl.ds(0, (KGROUPS[h][1] - KGROUPS[h][0]) * SUB)]
             remote(ref, ref, kv_s.at[k, h], kv_r.at[k, h], sib).wait_recv()
         return go
 
-    for h in range(2):
+    for h in range(len(KGROUPS)):
         for k in range(5):
             plan.token(f"k{k}{h}", wait_kv(k, h))
 
@@ -479,19 +516,22 @@
         def pass_two(h=h):
             kv_send(c, c, h, 4, sib)
 
-        plan.add(f"ka{h}", [f"k0{h}"], 0.1, 1, pass_one, [("zu", 2.2, 2.0, f"k1{h}"), ("cc", 0.3, 1.0, f"k3{h}")])
+        plan.add(f"ka{h}", [f"k0{h}"], 0.1, 1, pass_one, [("zu", kv_time(h), 2.0, f"k1{h}"), ("cc", 0.3, 1.0, f"k3{h}")])
         plan.add(f"kb{h}", [f"k1{h}"], 0.1, 1, pass_two, [("cc", 0.3, 1.0, f"k4{h}")])
-        for j in range(NCH):
+    for j in range(NCH):
+        for h in range(len(sent(j))):
             other_task(h, j)
+        for h in range(len(groups(j))):
             own_product(h, j)
             finish(h, j)
-    window_in = [f"k{k}{h}" for k in (2, 3, 4) for h in range(2)] + [f"done:kb{h}" for h in range(2)] + [f"done:f{h}0" for h in range(2)]
+    ngk = len(KGROUPS)
+    window_in = [f"k{k}{h}" for k in (2, 3, 4) for h in range(ngk)] + [f"done:kb{h}" for h in range(ngk)] + [f"done:f{h}0" for h in range(ngk)]
 
     def attend(j):
         def go():
-            row = lax.broadcasted_iota(jnp.int32, (HD, HD), 0)
-            col = lax.broadcasted_iota(jnp.int32, (HD, HD), 1)
-            later = col > row
+            row = lax.broadcasted_iota(jnp.int32, (2 * HD, HD), 0)
+            col = lax.broadcasted_iota(jnp.int32, (2 * HD, HD), 1)
+            later = col > row % HD
             key_at = lax.broadcasted_iota(jnp.int32, (1, WIN), 1)
 
             def block(b, carry):
@@ -500,27 +540,28 @@
                 keys = kvf[pl.ds(k0, WIN), 0:HD]
                 vals = kvf[pl.ds(k0, WIN), HD:2 * HD]
                 real = key_at >= (STEPS - ci) * TOK - b * HD
-                for half in range(2):
-                    q = qbuf[j - 1, pl.ds(r0, HD), half * HD:(half + 1) * HD]
-                    s = lax.dot_general(q, keys, (((1,), (1,)), ((), ())), preferred_element_type=F32)
-                    s = jnp.concatenate(
-                        [
-                            jnp.where(later, s[:, :HD], NEG),
-                            s[:, HD:WIN - HD],
-                            jnp.where(later, NEG, s[:, WIN - HD:]),
-                        ],
-                        axis=1,
-                    )
-                    s = jnp.where(real, s, NEG)
-                    peak = jnp.max(s, axis=1, keepdims=True)
-                    e = jnp.exp2((s - peak) * EXP_SCALE)
-                    probs = (e * (1.0 / jnp.sum(e, axis=1, keepdims=True))).astype(BF16)
-                    o = jnp.dot(probs, vals, preferred_element_type=F32)
-                    out[j - 1, pl.ds(r0, HD), half * HD:(half + 1) * HD] = o.astype(BF16)
+                q = jnp.concatenate(
+                    [qbuf[j - 1, pl.ds(r0, HD), 0:HD], qbuf[j - 1, pl.ds(r0, HD), HD:2 * HD]], axis=0
+                )
+                s = lax.dot_general(q, keys, (((1,), (1,)), ((), ())), preferred_element_type=F32)
+                s = jnp.concatenate(
+                    [
+                        jnp.where(later, s[:, :HD], NEG),
+                        s[:, HD:WIN - HD],
+                        jnp.where(later, NEG, s[:, WIN - HD:]),
+                    ],
+                    axis=1,
+                )
+                s = jnp.where(real, s, NEG)
+                peak = jnp.max(s, axis=1, keepdims=True)
+                e = jnp.exp2((s - peak) * EXP_SCALE)
+                probs = (e * (1.0 / jnp.sum(e, axis=1, keepdims=True))).astype(BF16)
+                o = jnp.dot(probs, vals, preferred_element_type=F32).astype(BF16)
+                o_ref[pl.ds(r0, HD), (j - 1) * 256:(j - 1) * 256 + HD] = o[:HD]
+                o_ref[pl.ds(r0, HD), (j - 1) * 256 + HD:j * 256] = o[HD:]
                 return carry
 
-            lax.fori_loop(0, TOK // HD, block, 0)
-            pltpu.make_async_copy(out.at[j - 1], o_hbm.at[:, pl.ds((j - 1) * 256, 256)], o_s.at[j - 1]).start()
+            lax.fori_loop(0, TOK // HD, block, 0, unroll=True)
         plan.add(f"a{j}", window_in + [f"done:f{h}{j}" for h in range(2)], 3.0, 7 + j, go)
 
     kvf = kvb.reshape(6 * TOK, 2 * HD)
@@ -530,8 +571,6 @@
     plan.emit(start)
     body.total = plan.total
 
-    for j in range(1, NCH):
-        pltpu.make_async_copy(out.at[j - 1], o_hbm.at[:, pl.ds((j - 1) * 256, 256)], o_s.at[j - 1]).wait()
     for cp in started:
         cp.wait_send()
     for t in range(2):
@@ -556,21 +595,22 @@
     inverse = jnp.power(F32(500000.0), -(jnp.arange(0, HD, 2).astype(F32) / HD))
     angles = position[:, None] * inverse[None, :]
     cosine, sine = jnp.cos(angles), jnp.sin(angles)
-    cos2 = jnp.concatenate([cosine, cosine], axis=1)
-    sin2 = jnp.concatenate([-sine, sine], axis=1)
     gain = norm_gain.astype(F32).reshape(8, WID)
     any_ = pl.BlockSpec(memory_space=pl.ANY)
+    hbm = pl.BlockSpec(memory_space=pltpu.HBM)
     dma = pltpu.SemaphoreType.DMA
     result = pl.pallas_call(
         body,
         out_shape=jax.ShapeDtypeStruct((TOK, 1024), BF16),
         in_specs=[
-            any_, pl.BlockSpec(memory_space=pltpu.VMEM), any_, pl.BlockSpec(memory_space=pltpu.SMEM), any_, any_,
+            hbm, pl.BlockSpec(memory_space=pltpu.VMEM), hbm, pl.BlockSpec(memory_space=pltpu.SMEM), any_, any_,
         ],
-        out_specs=any_,
+        out_specs=pl.BlockSpec(memory_space=pltpu.VMEM),
         scratch_shapes=[
             pltpu.VMEM((TOK, WID), BF16),
             pltpu.VMEM((ROWS, 1280), BF16),
+            pltpu.VMEM((TOK, HD // 2), F32),
+            pltpu.VMEM((TOK, HD // 2), F32),
             pltpu.VMEM((TOK, HD), F32),
             pltpu.VMEM((TOK, HD), F32),
             pltpu.VMEM((2, 4, TOK, WID), BF16),
@@ -581,7 +621,6 @@
             pltpu.VMEM((NCH, TOK, 256), F32),
             pltpu.VMEM((4, TOK, 256), BF16),
             pltpu.VMEM((6, TOK, 256), BF16),
-            pltpu.VMEM((4, TOK, 256), BF16),
             pltpu.VMEM((8, 8, TOK), F32),
             pltpu.VMEM((2, 8, TOK), F32),
             pltpu.VMEM((2, TOK, HD), F32),
@@ -592,16 +631,15 @@
             dma((2, NSUB, 3)), dma((2, NSUB, 3)),
             dma((7,)), dma((7,)),
             dma((1,)), dma((1,)),
-            dma((NCH, 2)), dma((NCH, 2)),
-            dma((5, 2)), dma((5, 2)),
-            dma((4,)),
+            dma((NCH, 4)), dma((NCH, 4)),
+            dma((5, len(KGROUPS))), dma((5, len(KGROUPS))),
         ],
         compiler_params=pltpu.CompilerParams(
-            collective_id=0, has_side_effects=True, vmem_limit_bytes=58 * 2**20
+            collective_id=0, has_side_effects=True, vmem_limit_bytes=52 * 2**20
         ),
         cost_estimate=pl.CostEstimate(flops=12 * 10**9, bytes_accessed=3 * 10**6, transcendentals=6 * 10**6),
     )(
-        hidden_states, gain, qkv_weight.reshape(ROWS, 1280), block_mask.reshape(2, 10), cos2, sin2,
+        hidden_states, gain, qkv_weight.reshape(ROWS, 1280), block_mask.reshape(2, 10), cosine, sine,
     )
     return result.reshape(TOK, 1, 1024)
 

time: 121 us -> 112 us (0.926)
  Pallas kernels: 116 us -> 108 us
    pallas_call x1, Pallas kernels: 116 us -> 108 us  [shards(): pl.pallas_call(body, out_shape=jax.ShapeDtypeStruct((TOK, 1024), BF16), i...]
    unnamed x3 -> x7, local copies, waits for them, and re-layouts: 2.76 us -> 3.34 us
where the time goes in v3:
time: 112 us
  Pallas kernels  108 us (96%)
  local copies, waits for them, and re-layouts  3.35 us (3%)
    pallas_call x1, Pallas kernels, shards(): pl.pallas_call(body, out_shape=jax.ShapeDtypeStruct((TOK, 1024), BF16), i...  108 us
    unnamed x7, local copies, waits for them, and re-layouts  3.34 us

profile of v3, /device:TPU:1, one launch (start us, length us, event | category | flops | bytes accessed | tf_op | source)
XLA Modules:
  0.0 112.0 jit_solution(7619459266054456979)
XLA Ops:
  0.0 0.0 copy-start.2
  0.0 0.7 copy-done.2
  0.7 0.8 multiply_sine_fusion
  1.5 0.0 copy-start.1
  1.5 0.7 copy-done.1
  2.2 0.0 copy-start
  2.2 1.1 copy-done
  3.3 107.8 %shard_map.46 = bf16[384,1024]{1,0:T(8,128)(2,1)S(1)} custom-call(bf16[384,1024]{1,0:T(8,128)(2,1)} %x_hbm.1, f32[8,1024]{1,0:T(8,128)S(1)} %reshape.33.g_ref, bf16[256,1280]{1,0:T(8,128)(2,1)S(1)} %bitcast.4, s32[2,10]{1,0:T(2,128)S(1)} %bitcast.5, f32[384,64]{1,0:T(8,128)S(1)} %get-tuple-element.6.cos_hbm, f32[384,64]{1,0:T(8,128)S(1)} %get-tuple-element.5.sin_hbm), custom_call_target="tpu_custom_call" | custom-call | flops 12000000000 | bytes 3000000 | tf_op jit(solution)/shard_map/pallas_call | solution.py:602
  111.1 0.9 copy.6
  (3 shorter events, 0.0 us)
Async XLA Ops:
  0.0 0.7 copy-start.2
  1.5 0.7 copy-start.1
  2.2 1.1 copy-start

commit v4 on v3

--- a/solution.py
+++ b/solution.py
@@ -207,7 +207,7 @@
     def at(step):
         return ((z + 8 + step) % 8) * 2 + c
 
-    pz, lz = 2.9, 1.5
+    pz, lz = 3.1, 2.0
 
     def wait_w(j, way, d):
         def go():
@@ -275,7 +275,7 @@
         for j in range(NCH)
     ]
 
-    ph, lh = 2.2, 1.5
+    ph, lh = 2.35, 2.0
 
     def hpiece(t, yy, m):
         return hid.at[t, yy, hrows(m)]
@@ -444,8 +444,8 @@
         plan.token(f"p{j}{h}", wait_pr(j, h))
         deps = [f"done:n0{m}{s}" for m in range(lo, hi) for s in range(4)]
         plan.add(
-            f"m0{h}{j}", deps + chunk_in[j], 1.0 if hi - lo > 2 else 0.7, 5 + j * 0.1 + h * 0.01, go,
-            [("xp", 1.1 * (hi - lo), 2.0, f"p{j}{h}")],
+            f"m0{h}{j}", deps + chunk_in[j] + (["done:kb%d" % (len(KGROUPS) - 1)] if j == NCH - 1 else []), 1.0 if hi - lo > 2 else 0.7, 5 + j * 0.1 + h * 0.01, go,
+            [("xp", 1.2 * (hi - lo), 3.0, f"p{j}{h}")],
         )
 
     def rotated(u, rows):

time: 112 us -> 110 us (0.982)
  Pallas kernels: 108 us -> 105 us
    pallas_call x1, Pallas kernels: 108 us -> 105 us  [shards(): pl.pallas_call(body, out_shape=jax.ShapeDtypeStruct((TOK, 1024), BF16), i...]
where the time goes in v4:
time: 110 us; the launch traced here: 109 us
  Pallas kernels  105 us (95%)
  local copies, waits for them, and re-layouts  3.35 us (3%)
    pallas_call x1, Pallas kernels, shards(): pl.pallas_call(body, out_shape=jax.ShapeDtypeStruct((TOK, 1024), BF16), i...  105 us
    unnamed x7, local copies, waits for them, and re-layouts  3.34 us

profile of v4, /device:TPU:1, one launch (start us, length us, event | category | flops | bytes accessed | tf_op | source)
XLA Modules:
  0.0 109.4 jit_solution(10104995289042767936)
XLA Ops:
  0.0 0.0 copy-start.2
  0.0 0.7 copy-done.2
  0.7 0.8 multiply_sine_fusion
  1.5 0.0 copy-start.1
  1.5 0.7 copy-done.1
  2.2 0.0 copy-start
  2.2 1.1 copy-done
  3.3 105.2 %shard_map.46 = bf16[384,1024]{1,0:T(8,128)(2,1)S(1)} custom-call(bf16[384,1024]{1,0:T(8,128)(2,1)} %x_hbm.1, f32[8,1024]{1,0:T(8,128)S(1)} %reshape.33.g_ref, bf16[256,1280]{1,0:T(8,128)(2,1)S(1)} %bitcast.4, s32[2,10]{1,0:T(2,128)S(1)} %bitcast.5, f32[384,64]{1,0:T(8,128)S(1)} %get-tuple-element.6.cos_hbm, f32[384,64]{1,0:T(8,128)S(1)} %get-tuple-element.5.sin_hbm), custom_call_target="tpu_custom_call" | custom-call | flops 12000000000 | bytes 3000000 | tf_op jit(solution)/shard_map/pallas_call | solution.py:602
  108.5 0.9 copy.6
  (3 shorter events, 0.0 us)
Async XLA Ops:
  0.0 0.7 copy-start.2
  1.5 0.7 copy-start.1
  2.2 1.1 copy-start

commit v5 on v4

--- a/solution.py
+++ b/solution.py
@@ -452,7 +452,7 @@
         return u * cosv[rows, :] + pltpu.roll(u, 64, 1) * sinv[rows, :]
 
     def groups(j):
-        return KGROUPS if j == 0 else QGROUPS
+        return KGROUPS if j == 0 else QGROUPS if j < 3 else ((0, NSUB),)
 
     def own_product(h, j):
         lo, hi = groups(j)[h]
@@ -562,7 +562,7 @@
                 return carry
 
             lax.fori_loop(0, TOK // HD, block, 0, unroll=True)
-        plan.add(f"a{j}", window_in + [f"done:f{h}{j}" for h in range(2)], 3.0, 7 + j, go)
+        plan.add(f"a{j}", window_in + [f"done:f{h}{j}" for h in range(len(groups(j)))], 3.0, 7 + j, go)
 
     kvf = kvb.reshape(6 * TOK, 2 * HD)
     for j in range(1, NCH):

time: 110 us -> 110 us (level)
  no operation moved by 1% of the time
where the time goes in v5:
time: 110 us; the launch traced here: 109 us
  Pallas kernels  105 us (95%)
  local copies, waits for them, and re-layouts  3.35 us (3%)
    pallas_call x1, Pallas kernels, shards(): pl.pallas_call(body, out_shape=jax.ShapeDtypeStruct((TOK, 1024), BF16), i...  105 us
    unnamed x7, local copies, waits for them, and re-layouts  3.34 us

profile of v5, /device:TPU:1, one launch (start us, length us, event | category | flops | bytes accessed | tf_op | source)
XLA Modules:
  0.0 109.5 jit_solution(7781811151817887565)
XLA Ops:
  0.0 0.0 copy-start.2
  0.0 0.7 copy-done.2
  0.7 0.8 multiply_sine_fusion
  1.5 0.0 copy-start.1
  1.5 0.7 copy-done.1
  2.2 0.0 copy-start
  2.2 1.1 copy-done
  3.3 105.3 %shard_map.46 = bf16[384,1024]{1,0:T(8,128)(2,1)S(1)} custom-call(bf16[384,1024]{1,0:T(8,128)(2,1)} %x_hbm.1, f32[8,1024]{1,0:T(8,128)S(1)} %reshape.33.g_ref, bf16[256,1280]{1,0:T(8,128)(2,1)S(1)} %bitcast.4, s32[2,10]{1,0:T(2,128)S(1)} %bitcast.5, f32[384,64]{1,0:T(8,128)S(1)} %get-tuple-element.6.cos_hbm, f32[384,64]{1,0:T(8,128)S(1)} %get-tuple-element.5.sin_hbm), custom_call_target="tpu_custom_call" | custom-call | flops 12000000000 | bytes 3000000 | tf_op jit(solution)/shard_map/pallas_call | solution.py:602
  108.6 0.9 copy.6
  (3 shorter events, 0.0 us)
Async XLA Ops:
  0.0 0.7 copy-start.2
  1.5 0.7 copy-start.1
  2.2 1.1 copy-start
